TPU v7x, 32 devices: a whole 2x2x4 slice. The times are simulated.
32 devices in a mesh: lev: 8 (over y, x, core), lat: 4 (over z).
Axes of the slice: x: 2, y: 2, z: 4, core: 2. Of those that a mesh axis runs over, the one named last changes fastest.
Arguments:
- adjoint_in: float32 [8, 64, 16, 2048], P(None, 'lev', 'lat'), may hold values from -6 to 6
- courant_lon: float32 [64, 16, 2048], P('lev', 'lat'), may hold values from -0.24 to 0.24
- courant_lat: float32 [64, 16, 2048], P('lev', 'lat'), may hold values from -0.24 to 0.24, as said below
- mass_flux: float32 [16, 2048], P('lat'), may hold values from 0.1 to 0.9
- conv_band: int32 [2, 16, 2048], P(None, 'lat'), may hold values from 24 to 64, as said below
- diff_inverse: float32 [16, 4, 16, 16], P('lat'), may hold values from 0 to 1
- obs_values: float32 [8, 4, 4, 16, 64], P('lev', 'lat'), may hold values from -6 to 6
- obs_column: int32 [8, 4, 4, 16], P('lev', 'lat'), may hold values from 0 to 1023
- obs_count: int32 [8, 4, 4], P('lev', 'lat'), may hold values from 0 to 16, as said below
Outputs:
- adjoint_out: float32 [8, 64, 16, 2048], P(None, 'lev', 'lat')
Inputs may be any that keep to these rules, and one draw needn't show every extreme that they name: `courant_lat`: the south face of the first latitude row carries no flow. `conv_band`: bands hold 4 to 32 levels. `obs_count`: slots at and after the count hold padding. `obs_column`: several soundings may share a column.
All inputs are finite; a program needn't handle non-finite values.
Results may differ from a plain program's by a relative error of at most 0.00007.
Values sent between devices are 32-bit elements; how exact they have to be, the bound alone decides.
A program may use at most 128 MiB of HBM per device.

v0:
```python
import jax
import jax.numpy as jnp
from jax import lax
from jax.sharding import PartitionSpec as P

ADV_STEPS = 2


def from_behind(value, axis, steps):
    count = lax.axis_size(axis)
    initial, last = (max(0, -steps), min(count, count - steps))
    return lax.ppermute(value, axis, [(source, source + steps) for source in range(initial, last)])


def padded_2(cells, sides, width):
    for axis, dim in sides:
        count = lax.axis_size(axis)
        ends = count - 1
        head = lax.slice_in_dim(cells, 0, width, axis=dim)
        tail = lax.slice_in_dim(cells, cells.shape[dim] - width, cells.shape[dim], axis=dim)
        cells = jnp.concatenate(
            [
                lax.ppermute(tail, axis, [(i, (i + 1) % count) for i in range(ends)]),
                cells,
                lax.ppermute(head, axis, [((i + 1) % count, i) for i in range(ends)]),
            ],
            axis=dim,
        )
    return cells


def advect(padded_rows, lat_faces, lon_faces):
    row_total = lon_faces.shape[-2]
    center_rows = padded_rows[..., 1 : row_total + 1, :]
    northern = padded_rows[..., 2 : row_total + 2, :]
    southern = padded_rows[..., 0:row_total, :]
    face_south = lat_faces[..., 0:row_total, :]
    face_north = lat_faces[..., 1 : row_total + 1, :]
    face_east = jnp.roll(lon_faces, -1, axis=-1)
    eastern = jnp.roll(center_rows, -1, axis=-1)
    western = jnp.roll(center_rows, 1, axis=-1)
    flow_east = jnp.maximum(face_east, 0.0)
    flow_west = jnp.minimum(lon_faces, 0.0)
    flow_north = jnp.maximum(face_north, 0.0)
    flow_south = jnp.minimum(face_south, 0.0)
    center = 1.0 - flow_east + flow_west - flow_north + flow_south
    return (
        center_rows * center
        + eastern * flow_east
        - western * flow_west
        + northern * flow_north
        - southern * flow_south
    )


def body(
    adjoint_in,
    courant_lon,
    courant_lat,
    mass_flux,
    conv_band,
    diff_inverse,
    obs_values,
    obs_column,
    obs_count,
):
    tracer_count, level_count, row_count, lon_count = adjoint_in.shape
    lev_count = lax.axis_size("lev")
    lev_index = lax.axis_index("lev")
    north_faces = from_behind(courant_lat[:, :1], "lat", -1)
    lat_faces = jnp.concatenate([courant_lat, north_faces], axis=1)
    state = adjoint_in
    for substep in range(ADV_STEPS):
        padded = padded_2(state, (("lat", 2),), 1)
        state = advect(padded, lat_faces, courant_lon)
    received_values, received_column, received_count = (
        lax.all_to_all(obs_values, "lat", split_axis=2, concat_axis=2, tiled=True),
        lax.all_to_all(obs_column, "lat", split_axis=2, concat_axis=2, tiled=True),
        lax.all_to_all(obs_count, "lat", split_axis=2, concat_axis=2, tiled=True),
    )
    all_level_count = received_values.shape[-1]
    block_width = row_count * lon_count // lev_count
    slot_ids = lax.broadcasted_iota(jnp.int32, received_column.shape, 3)
    valid_slot = (slot_ids < received_count[..., None]).reshape(-1)
    column_ids = lax.broadcasted_iota(jnp.int32, (1, block_width), 1)
    one_hot = ((received_column.reshape(-1)[:, None] == column_ids) & valid_slot[:, None]).astype(
        jnp.float32
    )
    forcing = jnp.einsum(
        "sl,sc->lc",
        received_values.reshape(-1, all_level_count),
        one_hot,
        precision=lax.Precision.HIGHEST,
    )
    block_start = lev_index * block_width
    row_here = block_start // lon_count
    band_here = lax.dynamic_slice_in_dim(
        conv_band.reshape(2, row_count * lon_count), block_start, block_width, axis=1
    )
    kappa_here = lax.dynamic_slice_in_dim(
        mass_flux.reshape(row_count * lon_count), block_start, block_width, axis=0
    )
    inverse_here = lax.dynamic_index_in_dim(diff_inverse, row_here, axis=0, keepdims=False)
    block_count, block_size = (inverse_here.shape[0], inverse_here.shape[1])
    all_levels = lax.broadcasted_iota(jnp.int32, (all_level_count, 1), 0)
    inside = ((all_levels >= band_here[0][None]) & (all_levels < band_here[1][None])).astype(
        jnp.float32
    )
    counted = (band_here[1] - band_here[0]).astype(jnp.float32)
    flattened = state.reshape(tracer_count, level_count, row_count * lon_count)
    columns = lax.all_to_all(flattened, "lev", split_axis=2, concat_axis=1, tiled=True)
    item_count = columns.shape[0]
    band_mean = jnp.sum(columns * inside[None], axis=1) / counted
    mixed = columns + kappa_here * inside[None] * (band_mean[:, None] - columns)
    blocked = mixed.reshape(item_count, block_count, block_size, block_width)
    diffused = jnp.einsum("bij,tbjc->tbic", inverse_here, blocked, precision=lax.Precision.HIGHEST)
    diffused = diffused.reshape(item_count, all_level_count, block_width) + forcing[None]
    result = lax.all_to_all(diffused, "lev", split_axis=1, concat_axis=2, tiled=True)
    result = result.reshape(tracer_count, level_count, row_count, lon_count)
    return result


def solution(mesh):
    placed = (
        P(None, "lev", "lat", None),
        P("lev", "lat", None),
        P("lev", "lat", None),
        P("lat", None),
        P(None, "lat", None),
        P("lat", None, None, None),
        P("lev", "lat", None, None, None),
        P("lev", "lat", None, None),
        P("lev", "lat", None),
    )
    return jax.shard_map(
        body, mesh=mesh, in_specs=placed, out_specs=P(None, "lev", "lat", None), check_vma=False
    )
```

profile of v0, /device:TPU:0, one launch (start us, length us, event | category | flops | bytes accessed | tf_op | source)
XLA Modules:
  0.0 246.2 jit_solution(8214617660706582536)
XLA Ops:
  0.0 1.0 slice.87
  1.0 1.3 collective-permute-start
  2.3 2.8 %copy.38 = f32[8,8,4,2048]{3,1,2,0:T(8,128)S(1)} copy(f32[8,8,4,2048]{3,2,1,0:T(4,128)} %param.9) | data formatting | bytes 4194304 | tf_op args[0]
  5.1 1.0 fusion.33
  6.2 1.3 collective-permute-start.1
  7.5 7.0 %collective-permute-start.2 = (f32[8,8,1,2048]{3,1,2,0:T(8,128)}, f32[8,8,1,2048]{3,1,2,0:T(8,128)}, u32[]{:S(2)}, u32[]{:S(2)}) collective-permute-start(f32[8,8,1,2048]{3,1,2,0:T(8,128)} %get-tuple-element.22), channel_id=1, source_target_pairs={{0,1},{1,2},{2,3},{4,5},{5,6},{6,7},{8,9},{9,10},{10,11},{12,13},{... | collective-permute-start | bytes 1572872 | tf_op jit(solution)/shard_map/ppermute | solution.py:23
  15.1 4.7 %all-to-all-start.2 = ((s32[1,1,4]{1,0,2:T(1,128)}), s32[1,1,4]{1,0,2:T(1,128)S(1)}, u32[]{:S(2)}, u32[]{:S(2)}) async-start(s32[1,1,4]{1,0,2:T(1,128)} %copy.58), calls=%async_computation.2 | async-start | bytes 4096 | tf_op jit(solution)/shard_map/all_to_all | solution.py:79
  19.9 2.8 %fusion.32 = (f32[8,8,4,2047]{3,1,2,0:T(8,128)}, f32[8,8,4,2047]{3,1,2,0:T(8,128)}) fusion(f32[8,8,4,2048]{3,1,2,0:T(8,128)S(1)} %copy.38), kind=kLoop, calls=%fused_computation.54 | loop fusion | bytes 8384512 | tf_op jit(solution)/shard_map/jit(_roll_static)/slice | solution.py:41
  26.5 2.7 %fusion.5 = f32[8,8,4,2048]{3,1,2,0:T(8,128)S(1)} fusion(f32[8,8,4,2048]{3,1,2,0:T(8,128)S(1)} %copy.38, f32[8,8,1,2048]{3,1,2,0:T(8,128)} %collective-permute-done.2, f32[8,8,1,2048]{3,1,2,0:T(8,128)} %collective-permute-done.1, f32[8,8,4,1]{3,1,2,0:T(8,128)S(1)} %copy-done.6, f32[8,8,4,2047]{3,1,2,0:T(8,128)S(1)} %copy-done.3, ...), kind=kLoop, calls=%fused_computation.8 | loop fusion | flops 6815744 | bytes 10747904 | tf_op jit(solution)/shard_map/sub | solution.py:48
  29.4 1.3 collective-permute-start.3
  30.7 4.6 %collective-permute-start.4 = (f32[8,8,1,2048]{3,1,2,0:T(8,128)S(1)}, f32[8,8,1,2048]{3,1,2,0:T(8,128)S(1)}, u32[]{:S(2)}, u32[]{:S(2)}) collective-permute-start(f32[8,8,1,2048]{3,1,2,0:T(8,128)S(1)} %get-tuple-element.16), channel_id=1, source_target_pairs={{0,1},{1,2},{2,3},{4,5},{5,6},{6,7},{8,9},{9,10},{10,11},{12,13},{... | collective-permute-start | bytes 1572872 | tf_op jit(solution)/shard_map/ppermute | solution.py:23
  35.3 2.7 %fusion.29 = (f32[8,8,4,2047]{3,1,2,0:T(8,128)}, f32[8,8,4,2047]{3,1,2,0:T(8,128)}) fusion(f32[8,8,4,2048]{3,1,2,0:T(8,128)S(1)} %fusion.5), kind=kLoop, calls=%fused_computation.51 | loop fusion | bytes 8384512 | tf_op jit(solution)/shard_map/jit(_roll_static)/slice | solution.py:41
  38.1 4.2 %all-to-all-start.1 = ((s32[1,1,4,16]{3,1,0,2:T(1,128)}), s32[1,1,4,16]{3,1,0,2:T(1,128)S(1)}, u32[]{:S(2)}, u32[]{:S(2)}) async-start(s32[1,1,4,16]{3,1,0,2:T(1,128)} %bitcast.14), calls=%async_computation.1 | async-start | bytes 4096 | tf_op jit(solution)/shard_map/all_to_all | solution.py:78
  42.2 1.7 fusion.28
  44.0 3.7 %all-to-all-done.1 = s32[1,1,4,16]{3,1,0,2:T(1,128)S(1)} async-done(((s32[1,1,4,16]{3,1,0,2:T(1,128)}), s32[1,1,4,16]{3,1,0,2:T(1,128)S(1)}, u32[]{:S(2)}, u32[]{:S(2)}) %all-to-all-start.1) | async-done | bytes 288 | tf_op jit(solution)/shard_map/all_to_all | solution.py:78
  48.3 3.2 %all-to-all-start.3 = ((f32[4,1,1024]{2,1,0:T(1,128)}), f32[4,1,1024]{2,1,0:T(1,128)S(1)}, u32[]{:S(2)}, u32[]{:S(2)}) async-start(f32[4,1,1024]{2,1,0:T(1,128)} %reshape.206), calls=%async_computation.3 | async-start | bytes 32768 | tf_op jit(solution)/shard_map/all_to_all | solution.py:77
  51.6 0.8 copy-done.7
  52.6 5.5 %fusion.1 = f32[8,8,4,2048]{3,1,2,0:T(8,128)S(1)} fusion(f32[8,8,4,2048]{3,1,2,0:T(8,128)} %copy-done.1, f32[8,8,1,2048]{3,1,2,0:T(8,128)} %copy-done.8, f32[8,8,1,2048]{3,1,2,0:T(8,128)} %copy-done.7, f32[8,8,4,1]{3,1,2,0:T(8,128)} %get-tuple-element.12, f32[8,8,4,2047]{3,1,2,0:T(8,128)} %get-tuple-element.14, f32[8,8,4,2047]{3,1,2,0:T(8,128)} %get-tuple-element.13, ...), kind=kLoop, calls=%fused_computation.2 | loop fusion | flops 6815744 | bytes 10747904 | tf_op jit(solution)/shard_map/sub | solution.py:48
  58.1 15.9 %copy.52 = f32[8,8,8192]{1,0,2:T(8,128)} copy(f32[8,8,8192]{2,1,0:T(8,128)S(1)} %bitcast.57) | data formatting | bytes 4194304 | tf_op jit(solution)/shard_map/reshape | solution.py:110
  74.0 21.0 %reshape.204 = f32[8,1,65536]{2,1,0:T(1,128)} reshape(f32[8192,8,8]{2,1,0:T(8,128)} %bitcast.55) | data formatting | bytes 4194304
  95.1 4.8 %all-to-all-start = ((f32[8,1,65536]{2,1,0:T(1,128)}), f32[8,1,65536]{2,1,0:T(1,128)}, u32[]{:S(2)}, u32[]{:S(2)}) async-start(f32[8,1,65536]{2,1,0:T(1,128)} %reshape.204), calls=%async_computation | async-start | bytes 4194304 | tf_op jit(solution)/shard_map/all_to_all | solution.py:111
  103.6 22.6 %all-to-all-done = f32[8,1,65536]{2,1,0:T(1,128)} async-done(((f32[8,1,65536]{2,1,0:T(1,128)}), f32[8,1,65536]{2,1,0:T(1,128)}, u32[]{:S(2)}, u32[]{:S(2)}) %all-to-all-start) | async-done | bytes 2097184 | tf_op jit(solution)/shard_map/all_to_all | solution.py:111
  126.2 7.2 %reduce.6 = f32[8,65536]{1,0:T(8,128)S(1)} reduce(f32[8,1,65536]{2,1,0:T(1,128)} %all-to-all-done, f32[]{:T(128)} %broadcast.151), dimensions={1}, to_apply=%all_to_all.35.reduce_sub_computation | reduce | bytes 4194308 | tf_op jit(solution)/shard_map/all_to_all | solution.py:111
  133.4 39.0 %reshape.205 = f32[8192,8,8]{2,1,0:T(8,128)} reshape(f32[8,65536]{1,0:T(8,128)S(1)} %reduce.6) | data formatting | bytes 4194304
  172.4 16.2 %copy.64 = f32[8,8,8,1024]{3,2,1,0:T(8,128)} copy(f32[8,8,8,1024]{1,0,3,2:T(8,128)} %bitcast.53) | data formatting | bytes 4194304 | tf_op jit(solution)/shard_map/all_to_all | solution.py:111
  188.7 19.1 %copy.54 = f32[8,8,8,1024]{3,2,1,0:T(8,128)S(1)} copy(f32[8,8,8,1024]{2,0,3,1:T(8,128)} %bitcast.54) | data formatting | bytes 4194304 | tf_op jit(solution)/shard_map/all_to_all | solution.py:111
  207.7 1.9 fusion.13
  210.0 1.9 fusion.16
  212.5 1.2 copy.60
  213.8 29.0 %all_to_all.51 = f32[8,64,1024]{2,0,1:T(8,128)S(1)} all-to-all(f32[8,64,1024]{2,0,1:T(8,128)S(1)} %copy.60), channel_id=1, replica_groups=mesh['lev'=8,'lat'=4] {'lev'}, dimensions={1} | all-to-all | bytes 4194304 | tf_op jit(solution)/shard_map/all_to_all | solution.py:118
  242.8 1.2 copy.62
  244.0 2.0 reshape.192
  (81 shorter events, 10.1 us)
Async XLA Ops:
  0.0 210.0 %copy-start = (f32[4,4,16,16]{3,2,1,0:T(8,128)S(1)}, f32[4,4,16,16]{3,2,1,0:T(8,128)}, u32[]{:S(2)}) copy-start(f32[4,4,16,16]{3,2,1,0:T(8,128)} %param.14) | copy-start | bytes 49156
  1.0 23.3 %collective-permute-start = (f32[8,1,2048]{2,1,0:T(1,128)S(1)}, f32[8,1,2048]{2,1,0:T(1,128)S(1)}, u32[]{:S(2)}, u32[]{:S(2)}) collective-permute-start(f32[8,1,2048]{2,1,0:T(1,128)S(1)} %slice.87), channel_id=1, source_target_pairs={{1,0},{2,1},{3,2},{5,4},{6,5},{7,6},{9,8},{10,9},{11,10},{13,12},{... | collective-permute-start | bytes 196616 | tf_op jit(solution)/shard_map/ppermute | solution.py:12
  5.1 9.3 %copy-start.17 = (s32[1,1,4]{2,1,0:T(1,128)S(1)}, s32[1,1,4]{2,1,0:T(1,128)}, u32[]{:S(2)}) copy-start(s32[1,1,4]{2,1,0:T(1,128)} %param.17) | copy-start | bytes 52
  6.2 19.4 %collective-permute-start.1 = (f32[8,8,1,2048]{3,1,2,0:T(8,128)}, f32[8,8,1,2048]{3,1,2,0:T(8,128)}, u32[]{:S(2)}, u32[]{:S(2)}) collective-permute-start(f32[8,8,1,2048]{3,1,2,0:T(8,128)} %get-tuple-element.21), channel_id=1, source_target_pairs={{1,0},{2,1},{3,2},{5,4},{6,5},{7,6},{9,8},{10,9},{11,10},{13,12},{... | collective-permute-start | bytes 1572872 | tf_op jit(solution)/shard_map/ppermute | solution.py:25
  7.5 18.1 %collective-permute-start.2 = (f32[8,8,1,2048]{3,1,2,0:T(8,128)}, f32[8,8,1,2048]{3,1,2,0:T(8,128)}, u32[]{:S(2)}, u32[]{:S(2)}) collective-permute-start(f32[8,8,1,2048]{3,1,2,0:T(8,128)} %get-tuple-element.22), channel_id=1, source_target_pairs={{0,1},{1,2},{2,3},{4,5},{5,6},{6,7},{8,9},{9,10},{10,11},{12,13},{... | collective-permute-start | bytes 1572872 | tf_op jit(solution)/shard_map/ppermute | solution.py:23
  15.1 22.9 %all-to-all-start.2 = ((s32[1,1,4]{1,0,2:T(1,128)}), s32[1,1,4]{1,0,2:T(1,128)S(1)}, u32[]{:S(2)}, u32[]{:S(2)}) async-start(s32[1,1,4]{1,0,2:T(1,128)} %copy.58), calls=%async_computation.2 | async-start | bytes 4096 | tf_op jit(solution)/shard_map/all_to_all | solution.py:79
  19.9 3.5 %copy-start.11 = (f32[1,1,4,16,64]{4,3,2,1,0:T(8,128)S(1)}, f32[1,1,4,16,64]{4,3,2,1,0:T(8,128)}, u32[]{:S(2)}) copy-start(f32[1,1,4,16,64]{4,3,2,1,0:T(8,128)} %param.15) | copy-start | bytes 49156
  19.9 3.5 %copy-start.4 = (f32[8,4,2048]{2,1,0:T(4,128)S(1)}, f32[8,4,2048]{2,1,0:T(4,128)}, u32[]{:S(2)}) copy-start(f32[8,4,2048]{2,1,0:T(4,128)} %param.10) | copy-start | bytes 786436
  19.9 4.5 %slice-start = ((f32[8,4,2048]{2,1,0:T(4,128)}), f32[8,4,1]{2,1,0:T(4,128)S(1)}, s32[]{:S(2)}) async-start(f32[8,4,2048]{2,1,0:T(4,128)} %param.10), calls=%async_computation.5 | async-start | bytes 32768 | tf_op jit(solution)/shard_map/jit(_roll_static)/slice | solution.py:39
  19.9 4.5 %copy-start.9 = (f32[8,4,2048]{2,1,0:T(4,128)S(1)}, f32[8,4,2048]{2,1,0:T(4,128)}, u32[]{:S(2)}) copy-start(f32[8,4,2048]{2,1,0:T(4,128)} %param.11) | copy-start | bytes 786436
  24.3 1.6 copy-start.2
  24.3 2.2 copy-start.3
  24.3 2.2 copy-start.5
  24.3 2.2 copy-start.6
  29.3 6.0 %copy-start.1 = (f32[8,8,4,2048]{3,1,2,0:T(8,128)}, f32[8,8,4,2048]{3,1,2,0:T(8,128)S(1)}, u32[]{:S(2)}) copy-start(f32[8,8,4,2048]{3,1,2,0:T(8,128)S(1)} %fusion.5) | copy-start | bytes 6291460
  29.4 22.2 %collective-permute-start.3 = (f32[8,8,1,2048]{3,1,2,0:T(8,128)S(1)}, f32[8,8,1,2048]{3,1,2,0:T(8,128)S(1)}, u32[]{:S(2)}, u32[]{:S(2)}) collective-permute-start(f32[8,8,1,2048]{3,1,2,0:T(8,128)S(1)} %get-tuple-element.15), channel_id=1, source_target_pairs={{1,0},{2,1},{3,2},{5,4},{6,5},{7,6},{9,8},{10,9},{11,10},{13,12},{... | collective-permute-start | bytes 1572872 | tf_op jit(solution)/shard_map/ppermute | solution.py:25
  30.7 20.9 %collective-permute-start.4 = (f32[8,8,1,2048]{3,1,2,0:T(8,128)S(1)}, f32[8,8,1,2048]{3,1,2,0:T(8,128)S(1)}, u32[]{:S(2)}, u32[]{:S(2)}) collective-permute-start(f32[8,8,1,2048]{3,1,2,0:T(8,128)S(1)} %get-tuple-element.16), channel_id=1, source_target_pairs={{0,1},{1,2},{2,3},{4,5},{5,6},{6,7},{8,9},{9,10},{10,11},{12,13},{... | collective-permute-start | bytes 1572872 | tf_op jit(solution)/shard_map/ppermute | solution.py:23
  38.1 9.7 %copy-start.13 = (s32[1,1,4]{1,0,2:T(1,128)}, s32[1,1,4]{1,0,2:T(1,128)S(1)}, u32[]{:S(2)}) copy-start(s32[1,1,4]{1,0,2:T(1,128)S(1)} %all-to-all-done.2) | copy-start | bytes 52
  38.1 9.7 %all-to-all-start.1 = ((s32[1,1,4,16]{3,1,0,2:T(1,128)}), s32[1,1,4,16]{3,1,0,2:T(1,128)S(1)}, u32[]{:S(2)}, u32[]{:S(2)}) async-start(s32[1,1,4,16]{3,1,0,2:T(1,128)} %bitcast.14), calls=%async_computation.1 | async-start | bytes 4096 | tf_op jit(solution)/shard_map/all_to_all | solution.py:78
  47.7 0.6 copy-start.15
  48.3 46.7 %all-to-all-start.3 = ((f32[4,1,1024]{2,1,0:T(1,128)}), f32[4,1,1024]{2,1,0:T(1,128)S(1)}, u32[]{:S(2)}, u32[]{:S(2)}) async-start(f32[4,1,1024]{2,1,0:T(1,128)} %reshape.206), calls=%async_computation.3 | async-start | bytes 32768 | tf_op jit(solution)/shard_map/all_to_all | solution.py:77
  51.6 0.8 copy-start.7
  51.6 1.0 copy-start.8
  95.0 4.8 %copy-start.10 = (s32[2,4,2048]{2,1,0:T(4,128)S(1)}, s32[2,4,2048]{2,1,0:T(4,128)}, u32[]{:S(2)}) copy-start(s32[2,4,2048]{2,1,0:T(4,128)} %param.13) | copy-start | bytes 196612
  95.0 4.9 %copy-start.12 = (f32[4,2048]{1,0:T(4,128)S(1)}, f32[4,2048]{1,0:T(4,128)}, u32[]{:S(2)}) copy-start(f32[4,2048]{1,0:T(4,128)} %param.12) | copy-start | bytes 98308
  95.0 5.3 %copy-start.14 = (s32[1,1,4]{1,0,2:T(1,128)S(1)}, s32[1,1,4]{1,0,2:T(1,128)}, u32[]{:S(2)}) copy-start(s32[1,1,4]{1,0,2:T(1,128)} %copy-done.13) | copy-start | bytes 52
  95.0 6.2 %copy-start.16 = (s32[1,1,4,16]{3,1,0,2:T(1,128)S(1)}, s32[1,1,4,16]{3,1,0,2:T(1,128)}, u32[]{:S(2)}) copy-start(s32[1,1,4,16]{3,1,0,2:T(1,128)} %copy-done.15) | copy-start | bytes 772
  95.1 31.2 %all-to-all-start = ((f32[8,1,65536]{2,1,0:T(1,128)}), f32[8,1,65536]{2,1,0:T(1,128)}, u32[]{:S(2)}, u32[]{:S(2)}) async-start(f32[8,1,65536]{2,1,0:T(1,128)} %reshape.204), calls=%async_computation | async-start | bytes 4194304 | tf_op jit(solution)/shard_map/all_to_all | solution.py:111
where the time goes:
time: 251 us; the launch traced here: 246 us
  local copies, waits for them, and re-layouts  135 us (54%)
  starting transfers between devices  32.4 us (13%)
  blocking collectives  29 us (12%)
  waiting for transfers between devices  26.3 us (10%)
  other arithmetic  20.3 us (8%)
    unnamed x45, local copies, waits for them, and re-layouts  66.9 us
    all_to_all x3, local copies, waits for them, and re-layouts, body(): lax.all_to_all(flattened, 'lev', split_axis=2, concat_axis=1, tiled=True)  35.8 us
    all_to_all x1, blocking collectives, body(): lax.all_to_all(diffused, 'lev', split_axis=1, concat_axis=2, tiled=True)  29 us
    all_to_all x1, waiting for transfers between devices, body(): lax.all_to_all(flattened, 'lev', split_axis=2, concat_axis=1, tiled=True)  22.6 us
    reshape x1, local copies, waits for them, and re-layouts, body(): flattened = state.reshape(tracer_count, level_count, row_count * lon_count)  15.9 us
    ppermute x2, starting transfers between devices, padded_2(): lax.ppermute(tail, axis, [(i, (i + 1) % count) for i in range(ends)])  11.6 us
    sub x2, other arithmetic, advect(): center_rows * center + eastern * flow_east - western * flow_west  8.26 us
    slice x4, local copies, waits for them, and re-layouts, advect(): western = jnp.roll(center_rows, 1, axis=-1)  8.01 us
  transfers between devices with their start and end apart: 9, of which 2 were waited for; matrix products, arithmetic and copies ran while one was open for 26% of the time, Pallas kernels for 0%

commit v1 on v0

v1 whole, which is shorter than its diff:
```python
import functools

import jax
import jax.numpy as jnp
from jax import lax
from jax.experimental import pallas as pl
from jax.experimental.pallas import tpu as pltpu
from jax.sharding import PartitionSpec as P

MESH = pl.DeviceIdType.MESH
LANES = 128


def kernel(
    lev_n, lat_n,
    a_ref, u_ref, v_ref, band_ref, flux_ref, diff_ref, obs_ref,
    out_ref,
    a1, a2, a2o, halo0, halo1, vnorth, cc, fe, fw, fn, fs,
    io, ip, go, gp, mx, bs, bsr, bmean, force, obs_in, msg, got,
    s_obs1, r_obs1, s_obs2, r_obs2, s_v, r_v, s_h0, r_h0, s_h1, r_h1, s_pair, r_pair, s_bs, r_bs,
):
    T, R, C, L, _ = a_ref.shape
    lev = lax.axis_index("lev")
    lat = lax.axis_index("lat")
    chips = lev_n // 2
    partner = lev + 1 - 2 * (lev % 2)
    has_north = lat < lat_n - 1
    has_south = lat > 0
    tiles = R * C // lev_n
    levels = lev_n * L

    def remote(src, dst, s, r, dev):
        return pltpu.make_async_remote_copy(
            src_ref=src, dst_ref=dst, send_sem=s, recv_sem=r, device_id=dev, device_id_type=MESH
        )

    def obs1(d):
        to = (lat + d) % lat_n
        return remote(obs_ref.at[to], obs_in.at[d - 1], s_obs1.at[d - 1], r_obs1.at[d - 1], (lev, to))

    def obs2(d):
        to = (lev + d) % lev_n
        return remote(msg.at[to], got.at[lev], s_obs2.at[d - 1], r_obs2.at[d - 1], (to, lat))

    def obs2_wait(d):
        src = (lev - d + lev_n) % lev_n
        return remote(msg.at[src], got.at[src], s_obs2.at[d - 1], r_obs2.at[d - 1], (src, lat))

    def south(src, dst, s, r):
        return remote(src, dst, s, r, (lev, lax.max(lat - 1, 0)))

    def north(src, dst, s, r):
        return remote(src, dst, s, r, (lev, lax.min(lat + 1, lat_n - 1)))

    def v_copy():
        return south(v_ref.at[0], vnorth, s_v, r_v)

    def halo_south(src, dst, s, r, t):
        return south(src.at[t, 0], dst.at[1, t], s.at[1, t], r.at[1, t])

    def halo_north(src, dst, s, r, t):
        return north(src.at[t, R - 1], dst.at[0, t], s.at[0, t], r.at[0, t])

    def halo_send(src, dst, s, r, t):
        @pl.when(has_south)
        def _():
            halo_south(src, dst, s, r, t).start()

        @pl.when(has_north)
        def _():
            halo_north(src, dst, s, r, t).start()

    def halo_recv(src, dst, s, r, t):
        @pl.when(has_south)
        def _():
            halo_north(src, dst, s, r, t).wait_recv()

        @pl.when(has_north)
        def _():
            halo_south(src, dst, s, r, t).wait_recv()

    def halo_sent(src, dst, s, r, t):
        @pl.when(has_south)
        def _():
            halo_south(src, dst, s, r, t).wait_send()

        @pl.when(has_north)
        def _():
            halo_north(src, dst, s, r, t).wait_send()

    def pair(t):
        return remote(a2.at[t], a2o.at[t], s_pair.at[t], r_pair.at[t], (partner, lat))

    def sums(d, t):
        to = (lev + 2 * d) % lev_n
        return remote(bs.at[t], bsr.at[d - 1, t], s_bs.at[d - 1, t], r_bs.at[d - 1, t], (to, lat))

    barrier = pltpu.get_barrier_semaphore()
    for d in range(1, lat_n):
        pl.semaphore_signal(barrier, inc=1, device_id=(lev, (lat + d) % lat_n), device_id_type=MESH)
    for d in range(1, lev_n):
        pl.semaphore_signal(barrier, inc=1, device_id=((lev + d) % lev_n, lat), device_id_type=MESH)
    pl.semaphore_wait(barrier, lat_n + lev_n - 2)

    for d in range(1, lat_n):
        obs1(d).start()

    @pl.when(has_south)
    def _():
        v_copy().start()

    @pl.loop(0, T)
    def _(t):
        halo_send(a_ref, halo0, s_h0, r_h0, t)

    @pl.when(jnp.logical_not(has_south))
    def _():
        halo0[0] = jnp.zeros_like(halo0[0])
        halo1[0] = jnp.zeros_like(halo1[0])

    @pl.when(jnp.logical_not(has_north))
    def _():
        halo0[1] = jnp.zeros_like(halo0[1])
        halo1[1] = jnp.zeros_like(halo1[1])
        vnorth[...] = jnp.zeros_like(vnorth)

    lane = lax.broadcasted_iota(jnp.int32, (C, L, LANES), 2)

    def eastern(x):
        r = pltpu.roll(x, LANES - 1, 2)
        return jnp.where(lane == LANES - 1, jnp.concatenate([r[1:], r[:1]], axis=0), r)

    def western(x):
        r = pltpu.roll(x, 1, 2)
        return jnp.where(lane == 0, jnp.concatenate([r[-1:], r[:-1]], axis=0), r)

    level = lax.broadcasted_iota(jnp.int32, (L, LANES), 0)
    for r in range(R):
        for c in range(C):
            k = r * C + c
            lo = jnp.broadcast_to(band_ref[0, k : k + 1, :], (L, LANES))
            hi = jnp.broadcast_to(band_ref[1, k : k + 1, :], (L, LANES))
            kap = jnp.broadcast_to(flux_ref[k : k + 1, :], (L, LANES))
            for base, inside, g in ((lev * L, io, go), (partner * L, ip, gp)):
                here = jnp.where(level + base >= lo, 1.0, 0.0) * jnp.where(level + base < hi, 1.0, 0.0)
                inside[r, c] = here
                g[r, c] = kap * here

    @pl.when(has_north)
    def _():
        v_copy().wait_recv()

    for r in range(R):
        u = u_ref[r]
        e = jnp.maximum(eastern(u), 0.0)
        w = jnp.minimum(u, 0.0)
        n = jnp.maximum(v_ref[r + 1] if r < R - 1 else vnorth[...], 0.0)
        s = jnp.minimum(v_ref[r], 0.0)
        fe[r], fw[r], fn[r], fs[r] = e, w, n, s
        cc[r] = 1.0 - e + w - n + s

    def substep(src, halo, dst, t):
        for r in range(R):
            x = src[t, r]
            up = src[t, r + 1] if r < R - 1 else halo[1, t]
            down = src[t, r - 1] if r > 0 else halo[0, t]
            dst[t, r] = (
                x * cc[r] + eastern(x) * fe[r] - western(x) * fw[r] + up * fn[r] - down * fs[r]
            )

    for d in range(1, lat_n):
        obs1(d).wait_recv()
    total = obs_ref[lat]
    for d in range(1, lat_n):
        total = total + obs_in[d - 1]
    for i in range(lev_n):
        msg[i, 0:L] = total[i * L : (i + 1) * L]
        msg[i, L : 2 * L] = total[levels : levels + L]
    got[lev] = msg[lev]
    for d in range(1, lev_n):
        obs2(d).start()

    @pl.loop(0, T)
    def _(t):
        halo_recv(a_ref, halo0, s_h0, r_h0, t)
        substep(a_ref, halo0, a1, t)
        halo_send(a1, halo1, s_h1, r_h1, t)

    for d in range(1, lev_n):
        obs2_wait(d).wait_recv()
    width = got.shape[2]
    diagonal = lax.broadcasted_iota(jnp.int32, (width, width), 0) == lax.broadcasted_iota(
        jnp.int32, (width, width), 1
    )

    @pl.loop(0, lev_n)
    def _(i):
        values = got[i, 0:L]
        row = got[i, L : 2 * L][0:1]
        column = jnp.sum(jnp.where(diagonal, jnp.broadcast_to(row, (width, width)), 0.0), axis=1, keepdims=True)
        column = column.astype(jnp.int32) - 1
        high = values.astype(jnp.bfloat16).astype(jnp.float32)
        rest = values - high
        middle = rest.astype(jnp.bfloat16).astype(jnp.float32)
        parts = jnp.concatenate([high, middle, rest - middle, jnp.zeros_like(high)], axis=0).astype(jnp.bfloat16)
        for c in range(tiles):
            ids = lax.broadcasted_iota(jnp.int32, (width, LANES), 1) + c * LANES
            hot = jnp.where(column == ids, 1.0, 0.0).astype(jnp.bfloat16)
            f = jnp.dot(parts, hot, preferred_element_type=jnp.float32)
            force[i * tiles + c] = f[0:L] + f[L : 2 * L] + f[2 * L : 3 * L]

    counted = (band_ref[1] - band_ref[0]).astype(jnp.float32)

    def stage_a(t):
        halo_recv(a1, halo1, s_h1, r_h1, t)
        substep(a1, halo1, a2, t)
        pair(t).start()

    def stage_b(t):
        pair(t).wait_recv()
        for r in range(R):
            x = a2[t, r] * io[r] + a2o[t, r] * ip[r]
            bs[t, r * C : (r + 1) * C, :] = jnp.sum(x, axis=1)
        for d in range(1, chips):
            sums(d, t).start()

    def stage_c(t):
        acc = bs[t]
        for d in range(1, chips):
            sums(d, t).wait_recv()
            acc = acc + bsr[d - 1, t]
        bmean[...] = acc / counted
        for r in range(R):
            for c in range(C):
                k = r * C + c
                m = jnp.broadcast_to(bmean[k : k + 1, :], (L, LANES))
                x = a2[t, r, c]
                y = a2o[t, r, c]
                mx[r, c, 0:L] = x + go[r, c] * (m - x)
                mx[r, c, L : 2 * L] = y + gp[r, c] * (m - y)
        for r in range(R):
            acc = force[r * C : (r + 1) * C]
            for j in range(2 * L):
                acc = acc + diff_ref[r, j][None] * mx[r, :, j : j + 1, :]
            out_ref[t, r] = acc

    @pl.loop(0, T + 2)
    def _(s):
        @pl.when(s < T)
        def _():
            stage_a(s)

        @pl.when(jnp.logical_and(s >= 1, s < T + 1))
        def _():
            stage_b(s - 1)

        @pl.when(s >= 2)
        def _():
            stage_c(s - 2)

    for d in range(1, lat_n):
        obs1(d).wait_send()
    for d in range(1, lev_n):
        obs2(d).wait_send()

    @pl.when(has_south)
    def _():
        v_copy().wait_send()

    @pl.loop(0, T)
    def _(t):
        halo_sent(a_ref, halo0, s_h0, r_h0, t)
        halo_sent(a1, halo1, s_h1, r_h1, t)
        pair(t).wait_send()
        for d in range(1, chips):
            sums(d, t).wait_send()


def body(
    adjoint_in, courant_lon, courant_lat, mass_flux, conv_band, diff_inverse,
    obs_values, obs_column, obs_count,
):
    lev_n, lat_n = lax.axis_size("lev"), lax.axis_size("lat")
    lev, lat = lax.axis_index("lev"), lax.axis_index("lat")
    T, L, R, lon = adjoint_in.shape
    C = lon // LANES
    K = R * C
    levels, cap = obs_values.shape[-1], obs_values.shape[-2]

    a = adjoint_in.reshape(T, L, R, C, LANES).transpose(0, 2, 3, 1, 4)
    u = courant_lon.reshape(L, R, C, LANES).transpose(1, 2, 0, 3)
    v = courant_lat.reshape(L, R, C, LANES).transpose(1, 2, 0, 3)
    band = conv_band.reshape(2, K, LANES)
    flux = mass_flux.reshape(K, LANES)

    size = diff_inverse.shape[-1]
    block, first = lev * L // size, lev * L % size
    inverse = lax.dynamic_index_in_dim(diff_inverse, block, axis=1, keepdims=False)
    inverse = lax.dynamic_slice_in_dim(inverse, first, L, axis=1)
    inverse = jnp.where(first > 0, jnp.roll(inverse, -L, axis=2), inverse)
    diff = jnp.broadcast_to(inverse.transpose(0, 2, 1)[..., None], (R, size, L, LANES))

    width = -(-lat_n * cap // LANES) * LANES
    slots = lax.broadcasted_iota(jnp.int32, (lat_n, cap), 1)
    column = jnp.where(slots < obs_count[0, 0][:, None], obs_column[0, 0] + 1, 0).astype(jnp.float32)
    rows = jnp.concatenate(
        [obs_values[0, 0].transpose(0, 2, 1), jnp.broadcast_to(column[:, None], (lat_n, L, cap))], axis=1
    )
    obs = lax.dynamic_update_slice(
        jnp.zeros((lat_n, levels + L, width), jnp.float32), rows, (0, 0, lat * cap)
    )

    chips = lev_n // 2
    f32 = jnp.float32
    vm = lambda *shape: pltpu.VMEM(shape, f32)
    dma = lambda *shape: pltpu.SemaphoreType.DMA(shape)
    scratch = [
        vm(T, R, C, L, LANES), vm(T, R, C, L, LANES), vm(T, R, C, L, LANES),
        vm(2, T, C, L, LANES), vm(2, T, C, L, LANES), vm(C, L, LANES),
        *[vm(R, C, L, LANES)] * 9,
        vm(R, C, 2 * L, LANES), vm(T, K, LANES), vm(chips - 1, T, K, LANES), vm(K, LANES),
        vm(K, L, LANES), vm(lat_n - 1, levels + L, width), vm(lev_n, 2 * L, width), vm(lev_n, 2 * L, width),
        dma(lat_n - 1), dma(lat_n - 1), dma(lev_n - 1), dma(lev_n - 1),
        pltpu.SemaphoreType.DMA, pltpu.SemaphoreType.DMA,
        dma(2, T), dma(2, T), dma(2, T), dma(2, T), dma(T), dma(T), dma(chips - 1, T), dma(chips - 1, T),
    ]
    out = pl.pallas_call(
        functools.partial(kernel, lev_n, lat_n),
        out_shape=jax.ShapeDtypeStruct((T, R, C, L, LANES), f32),
        in_specs=[pl.BlockSpec(memory_space=pltpu.VMEM)] * 7,
        out_specs=pl.BlockSpec(memory_space=pltpu.VMEM),
        scratch_shapes=scratch,
        compiler_params=pltpu.CompilerParams(
            collective_id=0, has_side_effects=True, vmem_limit_bytes=44 * 1024 * 1024
        ),
    )(a, u, v, band, flux, diff, obs)
    return out.transpose(0, 3, 1, 2, 4).reshape(T, L, R, lon)


def solution(mesh):
    placed = (
        P(None, "lev", "lat", None),
        P("lev", "lat", None),
        P("lev", "lat", None),
        P("lat", None),
        P(None, "lat", None),
        P("lat", None, None, None),
        P("lev", "lat", None, None, None),
        P("lev", "lat", None, None),
        P("lev", "lat", None),
    )
    return jax.shard_map(
        body, mesh=mesh, in_specs=placed, out_specs=P(None, "lev", "lat", None), check_vma=False
    )
```

time: 251 us -> 60.3 us (0.24); the launches traced: 246 us -> 59.8 us
  local copies, waits for them, and re-layouts: 135 us -> 11 us
  Pallas kernels: 0 us -> 46.2 us
  starting transfers between devices: 32.4 us -> 0 us
  blocking collectives: 29 us -> 0 us
  waiting for transfers between devices: 26.3 us -> 0 us
  other arithmetic: 20.3 us -> 2.48 us
    unnamed x45 -> x2, local copies, waits for them, and re-layouts: 66.9 us -> 0.01 us
    pallas_call x0 -> x1, Pallas kernels: none -> 46.2 us  [body(): pl.pallas_call(functools.partial(kernel, lev_n, lat_n), out_shape=jax.Sha...]
    all_to_all x5 -> x0, local copies, waits for them, and re-layouts: 37.6 us -> none  [the longest x3 35.8 us: body(): lax.all_to_all(flattened, 'lev', split_axis=2, concat_axis=1, tiled=True)]
    all_to_all x1 -> x0, blocking collectives: 29 us -> none  [body(): lax.all_to_all(diffused, 'lev', split_axis=1, concat_axis=2, tiled=True)]
    all_to_all x4 -> x0, waiting for transfers between devices: 26.3 us -> none  [the longest x1 22.6 us: body(): lax.all_to_all(flattened, 'lev', split_axis=2, concat_axis=1, tiled=True)]
    all_to_all x4 -> x0, starting transfers between devices: 16.9 us -> none  [the longest x1 4.75 us: body(): lax.all_to_all(flattened, 'lev', split_axis=2, concat_axis=1, tiled=True)]
    ppermute x5 -> x0, starting transfers between devices: 15.4 us -> none  [the longest x2 11.6 us: padded_2(): lax.ppermute(tail, axis, [(i, (i + 1) % count) for i in range(ends)])]
    slice x10 -> x1, local copies, waits for them, and re-layouts: 10.4 us -> 0.07 us  [body(): inverse = jnp.where(first > 0, jnp.roll(inverse, -L, axis=2), inverse)]
  transfers between devices with their start and end apart: 9 -> 0, of which waited for: 2 -> 0; matrix products, arithmetic and copies ran while one was open for 26% -> 0% of each run, Pallas kernels for 0% -> 0%
where the time goes in v1:
time: 60.3 us; the launch traced here: 59.8 us
  Pallas kernels  46.2 us (77%)
  local copies, waits for them, and re-layouts  11 us (18%)
  other arithmetic  2.48 us (4%)
    pallas_call x1, Pallas kernels, body(): pl.pallas_call(functools.partial(kernel, lev_n, lat_n), out_shape=jax.Sha...  46.2 us
    reshape x2, local copies, waits for them, and re-layouts, body(): a = adjoint_in.reshape(T, L, R, C, LANES).transpose(0, 2, 3, 1, 4)  3.54 us
    reshape x1, local copies, waits for them, and re-layouts, body(): return out.transpose(0, 3, 1, 2, 4).reshape(T, L, R, lon)  2.68 us

profile of v1, /device:TPU:0, one launch (start us, length us, event | category | flops | bytes accessed | tf_op | source)
XLA Modules:
  0.0 59.8 jit_solution(134212363425793366)
XLA Ops:
  0.0 0.0 copy-start
  0.0 0.8 %fusion.1 = f32[4,16]{1,0:T(4,128)S(1)} fusion(s32[1,1,4,16]{3,2,1,0:T(4,128)} %param.16, s32[4]{0:T(128)} %bitcast.29), kind=kLoop, calls=%fused_computation.8 | loop fusion | flops 256 | bytes 528 | tf_op jit(solution)/shard_map/convert_element_type | solution.py:305
  0.8 0.8 %dynamic-slice_bitcast_fusion = f32[4,8,16]{2,1,0:T(8,128)S(1)} fusion(f32[4,4,16,16]{3,2,1,0:T(8,128)} %param.14, s32[]{:T(128)S(6)} %select_n.45, s32[]{:T(128)S(6)} %select_n.47), kind=kLoop, calls=%fused_computation.6 | loop fusion | bytes 4104 | tf_op jit(solution)/shard_map/dynamic_slice | solution.py:299
  1.6 0.1 fusion.2
  1.6 0.8 %fusion = f32[4,16,8]{1,2,0:T(8,128)S(1)} fusion(f32[4,8,8]{2,1,0:T(8,128)S(1)} %get-tuple-element.6, f32[4,8,8]{2,1,0:T(8,128)S(1)} %get-tuple-element.5, pred[]{:T(512)S(6)} %gt.3, f32[4,4,16,16]{3,2,1,0:T(8,128)} %param.14, s32[]{:T(128)S(6)} %select_n.45, s32[]{:T(128)S(6)} %select_n.47), kind=kLoop, calls=%fused_computation.5 | loop fusion | flops 1024 | bytes 6153 | tf_op jit(solution)/shard_map/transpose | solution.py:301
  2.5 0.1 copy.28
  2.6 0.1 broadcast_in_dim.22
  2.6 0.8 %pad_maximum_fusion = f32[4,72,16]{1,2,0:T(8,128)S(1)} fusion(f32[4,8,16]{1,2,0:T(8,128)S(1)} %broadcast_in_dim.22, f32[4,64,16]{1,2,0:T(8,128)} %bitcast.28), kind=kLoop, calls=%fused_computation.3 | loop fusion | flops 4608 | bytes 36864 | tf_op jit(solution)/shard_map/concatenate | solution.py:306
  3.5 0.8 %reshape.51.flux_ref = f32[64,128]{1,0:T(8,128)S(1)} reshape(f32[4,2048]{1,0:T(4,128)} %param.12) | data formatting | bytes 65536 | tf_op jit(solution)/shard_map/reshape | solution.py:294
  4.2 0.9 %reshape.50.band_ref = s32[2,64,128]{2,1,0:T(8,128)S(1)} reshape(s32[2,4,2048]{2,1,0:T(4,128)} %param.13) | data formatting | bytes 131072 | tf_op jit(solution)/shard_map/reshape | solution.py:293
  5.1 0.1 copy.29
  5.2 0.4 dynamic_update_slice.3.obs_ref
  5.6 0.1 broadcast_in_dim.10.diff_ref
  5.8 1.1 %reshape.54 = f32[8,4,16,128]{3,2,1,0:T(8,128)S(1)} reshape(f32[8,4,2048]{2,1,0:T(4,128)} %param.10) | data formatting | bytes 524288 | tf_op jit(solution)/shard_map/reshape | solution.py:291
  6.9 0.0 copy-done
  6.9 0.1 reshape.55
  7.0 0.3 copy_bitcast_fusion.1
  7.3 2.3 %reshape.53 = f32[8,8,4,16,128]{4,3,2,1,0:T(8,128)S(1)} reshape(f32[8,8,4,2048]{3,2,1,0:T(4,128)} %param.9) | data formatting | bytes 4194304 | tf_op jit(solution)/shard_map/reshape | solution.py:290
  9.7 1.2 %copy.41 = f32[8,8,4,16,128]{4,1,3,2,0:T(8,128)S(1)} copy(f32[8,8,4,16,128]{4,3,2,1,0:T(8,128)S(1)} %reshape.53) | data formatting | bytes 4194304 | tf_op jit(solution)/shard_map/reshape | solution.py:290
  10.9 46.2 %shard_map.91 = f32[8,4,16,8,128]{4,3,2,1,0:T(8,128)S(1)} custom-call(f32[8,4,16,8,128]{4,3,2,1,0:T(8,128)S(1)} %bitcast.26, f32[4,16,8,128]{3,2,1,0:T(8,128)S(1)} %get-tuple-element.8.u_ref, f32[4,16,8,128]{3,2,1,0:T(8,128)S(1)} %get-tuple-element.7.v_ref, s32[2,64,128]{2,1,0:T(8,128)S(1)} %reshape.50.band_ref, f32[64,128]{1,0:T(8,128)S(1)} %reshape.51.flux_ref, ...), custom_call_target="tpu_custom_call" | custom-call | tf_op jit(solution)/shard_map/pallas_call | solution.py:327
  57.1 2.7 %copy.30 = f32[8,8,4,2048]{3,2,1,0:T(4,128)} copy(f32[8,8,4,2048]{3,1,2,0:T(8,128)S(1)} %bitcast.27) | data formatting | bytes 4194304 | tf_op jit(solution)/shard_map/reshape | solution.py:337
  (1 shorter events, 0.0 us)
Async XLA Ops:
  0.0 6.9 %copy-start = (f32[8,4,2048]{2,1,0:T(4,128)S(1)}, f32[8,4,2048]{2,1,0:T(4,128)}, u32[]{:S(2)}) copy-start(f32[8,4,2048]{2,1,0:T(4,128)} %param.11) | copy-start | bytes 786436

commit v2 on v1

--- a/solution.py
+++ b/solution.py
@@ -13,13 +13,18 @@
 
 def kernel(
     lev_n, lat_n,
-    a_ref, u_ref, v_ref, band_ref, flux_ref, diff_ref, obs_ref,
+    raw_a, raw_u, raw_v, band_ref, flux_ref, inv_ref, values_ref, column_ref, count_ref,
     out_ref,
+    stage, stage_u, stage_v, a_ref, u_ref, v_ref, diff_ref, obs_ref, counted,
     a1, a2, a2o, halo0, halo1, vnorth, cc, fe, fw, fn, fs,
-    io, ip, go, gp, mx, bs, bsr, bmean, force, obs_in, msg, got,
-    s_obs1, r_obs1, s_obs2, r_obs2, s_v, r_v, s_h0, r_h0, s_h1, r_h1, s_pair, r_pair, s_bs, r_bs,
+    io, go, gp, mx, ps, pr, hs, bsr, bmean, force, obs_in, msg, got,
+    c_a, c_u, c_v, s_obs1, r_obs1, s_obs2, r_obs2, s_v, r_v, s_h0, r_h0, s_h1, r_h1, s_pair, r_pair,
+    s_part, r_part, s_bs, r_bs, s_mean, r_mean,
 ):
     T, R, C, L, _ = a_ref.shape
+    K = R * C
+    H = K // 2
+    half = lax.axis_index("lev") % 2
     lev = lax.axis_index("lev")
     lat = lax.axis_index("lat")
     chips = lev_n // 2
@@ -28,6 +33,10 @@
     has_south = lat > 0
     tiles = R * C // lev_n
     levels = lev_n * L
+    cap = values_ref.shape[3]
+    first = pl.multiple_of(half * L, L)
+    mine = pl.ds(pl.multiple_of(half * H, H), H)
+    other = pl.ds(pl.multiple_of((1 - half) * H, H), H)
 
     def remote(src, dst, s, r, dev):
         return pltpu.make_async_remote_copy(
@@ -36,7 +45,7 @@
 
     def obs1(d):
         to = (lat + d) % lat_n
-        return remote(obs_ref.at[to], obs_in.at[d - 1], s_obs1.at[d - 1], r_obs1.at[d - 1], (lev, to))
+        return remote(obs_ref.at[to], obs_in.at[pl.ds(d * cap, cap)], s_obs1.at[d - 1], r_obs1.at[d - 1], (lev, to))
 
     def obs2(d):
         to = (lev + d) % lev_n
@@ -91,9 +100,31 @@
     def pair(t):
         return remote(a2.at[t], a2o.at[t], s_pair.at[t], r_pair.at[t], (partner, lat))
 
+    def part(t):
+        return remote(ps.at[t, other], pr.at[t], s_part.at[t], r_part.at[t], (partner, lat))
+
     def sums(d, t):
         to = (lev + 2 * d) % lev_n
-        return remote(bs.at[t], bsr.at[d - 1, t], s_bs.at[d - 1, t], r_bs.at[d - 1, t], (to, lat))
+        return remote(hs.at[t], bsr.at[d - 1, t], s_bs.at[d - 1, t], r_bs.at[d - 1, t], (to, lat))
+
+    def mean(t):
+        return remote(bmean.at[t, mine], bmean.at[t, mine], s_mean.at[t], r_mean.at[t], (partner, lat))
+
+    def mean_wait(t):
+        return remote(bmean.at[t, other], bmean.at[t, other], s_mean.at[t], r_mean.at[t], (partner, lat))
+
+    def load_a(t):
+        return pltpu.make_async_copy(raw_a.at[t], stage.at[t], c_a.at[t])
+
+    load_v = pltpu.make_async_copy(raw_v, stage_v, c_v)
+    load_u = pltpu.make_async_copy(raw_u, stage_u, c_u)
+    load_v.start()
+
+    @pl.loop(0, T)
+    def _(t):
+        load_a(t).start()
+
+    load_u.start()
 
     barrier = pltpu.get_barrier_semaphore()
     for d in range(1, lat_n):
@@ -102,8 +133,12 @@
         pl.semaphore_signal(barrier, inc=1, device_id=((lev + d) % lev_n, lat), device_id_type=MESH)
     pl.semaphore_wait(barrier, lat_n + lev_n - 2)
 
-    for d in range(1, lat_n):
-        obs1(d).start()
+    def tile(r, c):
+        return pl.ds(c * R + r, L, stride=K)
+
+    load_v.wait()
+    for c in range(C):
+        v_ref[0, c] = stage_v[tile(0, c), :]
 
     @pl.when(has_south)
     def _():
@@ -111,7 +146,46 @@
 
     @pl.loop(0, T)
     def _(t):
+        load_a(t).wait()
+        staged = stage.at[t]
+        for r in (0, R - 1):
+            for c in range(C):
+                a_ref[t, r, c] = staged[tile(r, c), :]
         halo_send(a_ref, halo0, s_h0, r_h0, t)
+
+    slot = lax.broadcasted_iota(jnp.int32, (cap, cap), 0)
+    across = lax.broadcasted_iota(jnp.int32, (cap, cap), 1)
+    for d in range(lat_n):
+        row = jnp.broadcast_to(column_ref[0, 0, d : d + 1, :], (cap, cap)).astype(jnp.float32) + 1.0
+        used = jnp.logical_and(slot == across, slot < count_ref[0, 0, d])
+        column = jnp.sum(jnp.where(used, row, 0.0), axis=1, keepdims=True)
+        obs_ref[d, :, 0:levels] = values_ref[0, 0, d]
+        obs_ref[d, :, levels:] = jnp.broadcast_to(column, (cap, obs_ref.shape[2] - levels))
+    for d in range(1, lat_n):
+        obs1(d).start()
+    obs_in[0:cap] = obs_ref[lat]
+    if obs_in.shape[0] > lat_n * cap:
+        obs_in[lat_n * cap :] = jnp.zeros_like(obs_in[lat_n * cap :])
+
+    @pl.loop(0, T)
+    def _(t):
+        staged = stage.at[t]
+        for r in range(1, R - 1):
+            for c in range(C):
+                a_ref[t, r, c] = staged[tile(r, c), :]
+
+    load_u.wait()
+    for r in range(R):
+        for c in range(C):
+            u_ref[r, c] = stage_u[tile(r, c), :]
+            if r > 0:
+                v_ref[r, c] = stage_v[tile(r, c), :]
+
+    block = lev * L // inv_ref.shape[3]
+    for r in range(R):
+        inverse = inv_ref[r, block, pl.ds(first, L), :]
+        for j in range(2 * L):
+            diff_ref[r, j] = jnp.broadcast_to(inverse[:, j : j + 1], (L, LANES))
 
     @pl.when(jnp.logical_not(has_south))
     def _():
@@ -138,13 +212,17 @@
     for r in range(R):
         for c in range(C):
             k = r * C + c
-            lo = jnp.broadcast_to(band_ref[0, k : k + 1, :], (L, LANES))
-            hi = jnp.broadcast_to(band_ref[1, k : k + 1, :], (L, LANES))
-            kap = jnp.broadcast_to(flux_ref[k : k + 1, :], (L, LANES))
-            for base, inside, g in ((lev * L, io, go), (partner * L, ip, gp)):
+            lon = slice(c * LANES, (c + 1) * LANES)
+            low, high = band_ref[0, r : r + 1, lon], band_ref[1, r : r + 1, lon]
+            counted[k : k + 1, :] = (high - low).astype(jnp.float32)
+            lo = jnp.broadcast_to(low, (L, LANES))
+            hi = jnp.broadcast_to(high, (L, LANES))
+            kap = jnp.broadcast_to(flux_ref[r : r + 1, lon], (L, LANES))
+            for base, g in ((lev * L, go), (partner * L, gp)):
                 here = jnp.where(level + base >= lo, 1.0, 0.0) * jnp.where(level + base < hi, 1.0, 0.0)
-                inside[r, c] = here
                 g[r, c] = kap * here
+                if g is go:
+                    io[r, c] = here
 
     @pl.when(has_north)
     def _():
@@ -170,9 +248,7 @@
 
     for d in range(1, lat_n):
         obs1(d).wait_recv()
-    total = obs_ref[lat]
-    for d in range(1, lat_n):
-        total = total + obs_in[d - 1]
+    total = jnp.transpose(obs_in[...])
     for i in range(lev_n):
         msg[i, 0:L] = total[i * L : (i + 1) * L]
         msg[i, L : 2 * L] = total[levels : levels + L]
@@ -209,54 +285,55 @@
             f = jnp.dot(parts, hot, preferred_element_type=jnp.float32)
             force[i * tiles + c] = f[0:L] + f[L : 2 * L] + f[2 * L : 3 * L]
 
-    counted = (band_ref[1] - band_ref[0]).astype(jnp.float32)
-
     def stage_a(t):
         halo_recv(a1, halo1, s_h1, r_h1, t)
         substep(a1, halo1, a2, t)
+        for r in range(R):
+            ps[t, r * C : (r + 1) * C, :] = jnp.sum(a2[t, r] * io[r], axis=1)
+        part(t).start()
         pair(t).start()
 
     def stage_b(t):
-        pair(t).wait_recv()
-        for r in range(R):
-            x = a2[t, r] * io[r] + a2o[t, r] * ip[r]
-            bs[t, r * C : (r + 1) * C, :] = jnp.sum(x, axis=1)
+        part(t).wait_recv()
+        hs[t] = ps[t, mine, :] + pr[t]
         for d in range(1, chips):
             sums(d, t).start()
 
     def stage_c(t):
-        acc = bs[t]
+        acc = hs[t]
         for d in range(1, chips):
             sums(d, t).wait_recv()
             acc = acc + bsr[d - 1, t]
-        bmean[...] = acc / counted
+        bmean[t, mine, :] = acc / counted[mine, :]
+        mean(t).start()
+
+    def stage_d(t):
+        pair(t).wait_recv()
+        mean_wait(t).wait_recv()
+        finished = out_ref.at[t]
         for r in range(R):
             for c in range(C):
                 k = r * C + c
-                m = jnp.broadcast_to(bmean[k : k + 1, :], (L, LANES))
+                m = jnp.broadcast_to(bmean[t, k : k + 1, :], (L, LANES))
                 x = a2[t, r, c]
                 y = a2o[t, r, c]
-                mx[r, c, 0:L] = x + go[r, c] * (m - x)
-                mx[r, c, L : 2 * L] = y + gp[r, c] * (m - y)
+                mx[r, c, pl.ds(first, L)] = x + go[r, c] * (m - x)
+                mx[r, c, pl.ds(L - first, L)] = y + gp[r, c] * (m - y)
         for r in range(R):
             acc = force[r * C : (r + 1) * C]
             for j in range(2 * L):
                 acc = acc + diff_ref[r, j][None] * mx[r, :, j : j + 1, :]
-            out_ref[t, r] = acc
-
-    @pl.loop(0, T + 2)
+            for c in range(C):
+                finished[tile(r, c), :] = acc[c]
+
+    stages = (stage_a, stage_b, stage_c, stage_d)
+
+    @pl.loop(0, T + len(stages) - 1)
     def _(s):
-        @pl.when(s < T)
-        def _():
-            stage_a(s)
-
-        @pl.when(jnp.logical_and(s >= 1, s < T + 1))
-        def _():
-            stage_b(s - 1)
-
-        @pl.when(s >= 2)
-        def _():
-            stage_c(s - 2)
+        for lag, run in enumerate(stages):
+            @pl.when(jnp.logical_and(s >= lag, s < T + lag))
+            def _():
+                run(s - lag)
 
     for d in range(1, lat_n):
         obs1(d).wait_send()
@@ -272,6 +349,8 @@
         halo_sent(a_ref, halo0, s_h0, r_h0, t)
         halo_sent(a1, halo1, s_h1, r_h1, t)
         pair(t).wait_send()
+        part(t).wait_send()
+        mean(t).wait_send()
         for d in range(1, chips):
             sums(d, t).wait_send()
 
@@ -281,60 +360,51 @@
     obs_values, obs_column, obs_count,
 ):
     lev_n, lat_n = lax.axis_size("lev"), lax.axis_size("lat")
-    lev, lat = lax.axis_index("lev"), lax.axis_index("lat")
     T, L, R, lon = adjoint_in.shape
     C = lon // LANES
     K = R * C
     levels, cap = obs_values.shape[-1], obs_values.shape[-2]
 
-    a = adjoint_in.reshape(T, L, R, C, LANES).transpose(0, 2, 3, 1, 4)
-    u = courant_lon.reshape(L, R, C, LANES).transpose(1, 2, 0, 3)
-    v = courant_lat.reshape(L, R, C, LANES).transpose(1, 2, 0, 3)
-    band = conv_band.reshape(2, K, LANES)
-    flux = mass_flux.reshape(K, LANES)
-
+    a = adjoint_in.reshape(T, L, R, C, LANES).transpose(0, 1, 3, 2, 4).reshape(T, L * K, LANES)
+    u = courant_lon.reshape(L, R, C, LANES).transpose(0, 2, 1, 3).reshape(L * K, LANES)
+    v = courant_lat.reshape(L, R, C, LANES).transpose(0, 2, 1, 3).reshape(L * K, LANES)
     size = diff_inverse.shape[-1]
-    block, first = lev * L // size, lev * L % size
-    inverse = lax.dynamic_index_in_dim(diff_inverse, block, axis=1, keepdims=False)
-    inverse = lax.dynamic_slice_in_dim(inverse, first, L, axis=1)
-    inverse = jnp.where(first > 0, jnp.roll(inverse, -L, axis=2), inverse)
-    diff = jnp.broadcast_to(inverse.transpose(0, 2, 1)[..., None], (R, size, L, LANES))
-
     width = -(-lat_n * cap // LANES) * LANES
-    slots = lax.broadcasted_iota(jnp.int32, (lat_n, cap), 1)
-    column = jnp.where(slots < obs_count[0, 0][:, None], obs_column[0, 0] + 1, 0).astype(jnp.float32)
-    rows = jnp.concatenate(
-        [obs_values[0, 0].transpose(0, 2, 1), jnp.broadcast_to(column[:, None], (lat_n, L, cap))], axis=1
-    )
-    obs = lax.dynamic_update_slice(
-        jnp.zeros((lat_n, levels + L, width), jnp.float32), rows, (0, 0, lat * cap)
-    )
+    depth = -(-(levels + L) // LANES) * LANES
 
     chips = lev_n // 2
     f32 = jnp.float32
     vm = lambda *shape: pltpu.VMEM(shape, f32)
     dma = lambda *shape: pltpu.SemaphoreType.DMA(shape)
     scratch = [
+        vm(T, L * K, LANES), vm(L * K, LANES), vm(L * K, LANES),
+        vm(T, R, C, L, LANES), vm(R, C, L, LANES), vm(R, C, L, LANES),
+        vm(R, size, L, LANES), vm(lat_n, cap, depth), vm(K, LANES),
         vm(T, R, C, L, LANES), vm(T, R, C, L, LANES), vm(T, R, C, L, LANES),
         vm(2, T, C, L, LANES), vm(2, T, C, L, LANES), vm(C, L, LANES),
-        *[vm(R, C, L, LANES)] * 9,
-        vm(R, C, 2 * L, LANES), vm(T, K, LANES), vm(chips - 1, T, K, LANES), vm(K, LANES),
-        vm(K, L, LANES), vm(lat_n - 1, levels + L, width), vm(lev_n, 2 * L, width), vm(lev_n, 2 * L, width),
+        *[vm(R, C, L, LANES)] * 8,
+        vm(R, C, 2 * L, LANES), vm(T, K, LANES), vm(T, K // 2, LANES), vm(T, K // 2, LANES),
+        vm(chips - 1, T, K // 2, LANES), vm(T, K, LANES),
+        vm(K, L, LANES), vm(width, depth), vm(lev_n, 2 * L, width), vm(lev_n, 2 * L, width),
+        dma(T), pltpu.SemaphoreType.DMA, pltpu.SemaphoreType.DMA,
         dma(lat_n - 1), dma(lat_n - 1), dma(lev_n - 1), dma(lev_n - 1),
         pltpu.SemaphoreType.DMA, pltpu.SemaphoreType.DMA,
-        dma(2, T), dma(2, T), dma(2, T), dma(2, T), dma(T), dma(T), dma(chips - 1, T), dma(chips - 1, T),
+        dma(2, T), dma(2, T), dma(2, T), dma(2, T), dma(T), dma(T), dma(T), dma(T),
+        dma(chips - 1, T), dma(chips - 1, T), dma(T), dma(T),
     ]
+    vmem = pl.BlockSpec(memory_space=pltpu.VMEM)
+    hbm = pl.BlockSpec(memory_space=pl.ANY)
     out = pl.pallas_call(
         functools.partial(kernel, lev_n, lat_n),
-        out_shape=jax.ShapeDtypeStruct((T, R, C, L, LANES), f32),
-        in_specs=[pl.BlockSpec(memory_space=pltpu.VMEM)] * 7,
+        out_shape=jax.ShapeDtypeStruct((T, L * K, LANES), f32),
+        in_specs=[hbm] * 3 + [vmem] * 5 + [pl.BlockSpec(memory_space=pltpu.SMEM)],
         out_specs=pl.BlockSpec(memory_space=pltpu.VMEM),
         scratch_shapes=scratch,
         compiler_params=pltpu.CompilerParams(
             collective_id=0, has_side_effects=True, vmem_limit_bytes=44 * 1024 * 1024
         ),
-    )(a, u, v, band, flux, diff, obs)
-    return out.transpose(0, 3, 1, 2, 4).reshape(T, L, R, lon)
+    )(a, u, v, conv_band, mass_flux, diff_inverse, obs_values, obs_column, obs_count)
+    return out.reshape(T, L, C, R, LANES).transpose(0, 1, 3, 2, 4).reshape(T, L, R, lon)
 
 
 def solution(mesh):

time: 60.3 us -> 57.6 us (0.955)
  other arithmetic: 2.48 us -> 0 us
  local copies, waits for them, and re-layouts: 11 us -> 9.4 us
  Pallas kernels: 46.2 us -> 47.5 us
    unnamed x2 -> x19, local copies, waits for them, and re-layouts: 0.01 us -> 9.4 us
    reshape x7 -> x0, local copies, waits for them, and re-layouts: 9.1 us -> none  [the longest x2 3.54 us: body(): a = adjoint_in.reshape(T, L, R, C, LANES).transpose(0, 2, 3, 1, 4)]
    pallas_call x1, Pallas kernels: 46.2 us -> 47.5 us  [body(): pl.pallas_call(functools.partial(kernel, lev_n, lat_n), out_shape=jax.Sha...]
    concatenate x1 -> x0, other arithmetic: 0.84 us -> none  [body(): jnp.concatenate([obs_values[0, 0].transpose(0, 2, 1), jnp.broadcast_to(co...]
    transpose x1 -> x0, other arithmetic: 0.84 us -> none  [body(): inverse.transpose(0, 2, 1)[..., None]]
    convert_element_type x1 -> x0, other arithmetic: 0.8 us -> none  [body(): jnp.where(slots < obs_count[0, 0][:, None], obs_column[0, 0] + 1, 0)]
    dynamic_slice x1 -> x0, local copies, waits for them, and re-layouts: 0.76 us -> none  [body(): inverse = lax.dynamic_slice_in_dim(inverse, first, L, axis=1)]
where the time goes in v2:
time: 57.6 us; the launch traced here: 56.9 us
  Pallas kernels  47.5 us (82%)
  local copies, waits for them, and re-layouts  9.4 us (16%)
    pallas_call x1, Pallas kernels, body(): pl.pallas_call(functools.partial(kernel, lev_n, lat_n), out_shape=jax.Sha...  47.5 us
    unnamed x19, local copies, waits for them, and re-layouts  9.4 us

profile of v2, /device:TPU:0, one launch (start us, length us, event | category | flops | bytes accessed | tf_op | source)
XLA Modules:
  0.0 56.9 jit_solution(911782890680080459)
XLA Ops:
  0.0 0.0 copy-start
  0.0 1.6 %copy-done = f32[8,8,4,2048]{3,2,1,0:T(4,128)S(1)} copy-done((f32[8,8,4,2048]{3,2,1,0:T(4,128)S(1)}, f32[8,8,4,2048]{3,2,1,0:T(4,128)}, u32[]{:S(2)}) %copy-start) | copy-done | bytes 2097176
  1.6 0.0 copy-start.1
  1.6 0.9 %copy-done.1 = f32[8,4,2048]{2,1,0:T(4,128)S(1)} copy-done((f32[8,4,2048]{2,1,0:T(4,128)S(1)}, f32[8,4,2048]{2,1,0:T(4,128)}, u32[]{:S(2)}) %copy-start.1) | copy-done | bytes 262168
  2.5 0.0 copy-start.2
  2.5 0.9 %copy-done.2 = f32[8,4,2048]{2,1,0:T(4,128)S(1)} copy-done((f32[8,4,2048]{2,1,0:T(4,128)S(1)}, f32[8,4,2048]{2,1,0:T(4,128)}, u32[]{:S(2)}) %copy-start.2) | copy-done | bytes 262168
  3.5 0.0 copy-start.3
  3.5 0.9 %copy-done.3 = f32[4,4,16,16]{3,2,1,0:T(8,128)S(1)} copy-done((f32[4,4,16,16]{3,2,1,0:T(8,128)S(1)}, f32[4,4,16,16]{3,2,1,0:T(8,128)}, u32[]{:S(2)}) %copy-start.3) | copy-done | bytes 16408
  4.4 0.0 copy-start.4
  4.4 0.8 %copy-done.4 = s32[2,4,2048]{2,1,0:T(4,128)S(1)} copy-done((s32[2,4,2048]{2,1,0:T(4,128)S(1)}, s32[2,4,2048]{2,1,0:T(4,128)}, u32[]{:S(2)}) %copy-start.4) | copy-done | bytes 65560
  5.2 0.0 copy-start.5
  5.2 0.8 %copy-done.5 = f32[4,2048]{1,0:T(4,128)S(1)} copy-done((f32[4,2048]{1,0:T(4,128)S(1)}, f32[4,2048]{1,0:T(4,128)}, u32[]{:S(2)}) %copy-start.5) | copy-done | bytes 32792
  6.0 0.0 copy-start.6
  6.0 0.8 %copy-done.6 = f32[1,1,4,16,64]{4,3,2,1,0:T(8,128)S(1)} copy-done((f32[1,1,4,16,64]{4,3,2,1,0:T(8,128)S(1)}, f32[1,1,4,16,64]{4,3,2,1,0:T(8,128)}, u32[]{:S(2)}) %copy-start.6) | copy-done | bytes 16408
  6.8 0.0 copy-start.7
  6.8 0.7 %copy-done.7 = s32[1,1,4,16]{3,2,1,0:T(4,128)S(1)} copy-done((s32[1,1,4,16]{3,2,1,0:T(4,128)S(1)}, s32[1,1,4,16]{3,2,1,0:T(4,128)}, u32[]{:S(2)}) %copy-start.7) | copy-done | bytes 280
  7.4 0.0 copy-start.8
  7.4 0.7 %copy-done.8 = s32[1,1,4]{2,1,0:T(1,128)S(1)} copy-done((s32[1,1,4]{2,1,0:T(1,128)S(1)}, s32[1,1,4]{2,1,0:T(1,128)}, u32[]{:S(2)}) %copy-start.8) | copy-done | bytes 40
  8.1 47.5 %shard_map.91 = f32[8,512,128]{2,1,0:T(8,128)S(1)} custom-call(f32[8,512,128]{2,1,0:T(8,128)S(1)} %bitcast.21, f32[512,128]{1,0:T(8,128)S(1)} %bitcast.22, f32[512,128]{1,0:T(8,128)S(1)} %bitcast.23, s32[2,4,2048]{2,1,0:T(4,128)S(1)} %copy-done.4, f32[4,2048]{1,0:T(4,128)S(1)} %copy-done.5, f32[4,4,16,16]{3,2,1,0:T(8,128)S(1)} %copy-done.3, ...), custom_call_target="tpu_custom_call" | custom-call | tf_op jit(solution)/shard_map/pallas_call | solution.py:397
  55.6 1.3 %copy.15 = f32[8,8,4,2048]{3,2,1,0:T(4,128)} copy(f32[8,8,4,2048]{3,2,1,0:T(4,128)S(1)} %bitcast.20) | data formatting | bytes 4194304
Async XLA Ops:
  0.0 1.6 %copy-start = (f32[8,8,4,2048]{3,2,1,0:T(4,128)S(1)}, f32[8,8,4,2048]{3,2,1,0:T(4,128)}, u32[]{:S(2)}) copy-start(f32[8,8,4,2048]{3,2,1,0:T(4,128)} %param.9) | copy-start | bytes 6291460
  1.6 0.9 %copy-start.1 = (f32[8,4,2048]{2,1,0:T(4,128)S(1)}, f32[8,4,2048]{2,1,0:T(4,128)}, u32[]{:S(2)}) copy-start(f32[8,4,2048]{2,1,0:T(4,128)} %param.10) | copy-start | bytes 786436
  2.5 0.9 %copy-start.2 = (f32[8,4,2048]{2,1,0:T(4,128)S(1)}, f32[8,4,2048]{2,1,0:T(4,128)}, u32[]{:S(2)}) copy-start(f32[8,4,2048]{2,1,0:T(4,128)} %param.11) | copy-start | bytes 786436
  3.5 0.9 %copy-start.3 = (f32[4,4,16,16]{3,2,1,0:T(8,128)S(1)}, f32[4,4,16,16]{3,2,1,0:T(8,128)}, u32[]{:S(2)}) copy-start(f32[4,4,16,16]{3,2,1,0:T(8,128)} %inv_ref.1) | copy-start | bytes 49156
  4.4 0.8 %copy-start.4 = (s32[2,4,2048]{2,1,0:T(4,128)S(1)}, s32[2,4,2048]{2,1,0:T(4,128)}, u32[]{:S(2)}) copy-start(s32[2,4,2048]{2,1,0:T(4,128)} %band_ref.1) | copy-start | bytes 196612
  5.2 0.8 %copy-start.5 = (f32[4,2048]{1,0:T(4,128)S(1)}, f32[4,2048]{1,0:T(4,128)}, u32[]{:S(2)}) copy-start(f32[4,2048]{1,0:T(4,128)} %flux_ref.1) | copy-start | bytes 98308
  6.0 0.8 %copy-start.6 = (f32[1,1,4,16,64]{4,3,2,1,0:T(8,128)S(1)}, f32[1,1,4,16,64]{4,3,2,1,0:T(8,128)}, u32[]{:S(2)}) copy-start(f32[1,1,4,16,64]{4,3,2,1,0:T(8,128)} %values_ref.1) | copy-start | bytes 49156
  6.8 0.7 %copy-start.7 = (s32[1,1,4,16]{3,2,1,0:T(4,128)S(1)}, s32[1,1,4,16]{3,2,1,0:T(4,128)}, u32[]{:S(2)}) copy-start(s32[1,1,4,16]{3,2,1,0:T(4,128)} %column_ref.1) | copy-start | bytes 772
  7.4 0.7 %copy-start.8 = (s32[1,1,4]{2,1,0:T(1,128)S(1)}, s32[1,1,4]{2,1,0:T(1,128)}, u32[]{:S(2)}) copy-start(s32[1,1,4]{2,1,0:T(1,128)} %count_ref.1) | copy-start | bytes 52

commit v3 on v2

--- a/solution.py
+++ b/solution.py
@@ -13,12 +13,13 @@
 
 def kernel(
     lev_n, lat_n,
-    raw_a, raw_u, raw_v, band_ref, flux_ref, inv_ref, values_ref, column_ref, count_ref,
+    raw_a, raw_u, raw_v, raw_band, raw_flux, raw_inv, raw_values, raw_column, raw_count,
     out_ref,
+    band_ref, flux_ref, inv_ref, values_ref, column_ref, count_ref,
     stage, stage_u, stage_v, a_ref, u_ref, v_ref, diff_ref, obs_ref, counted,
     a1, a2, a2o, halo0, halo1, vnorth, cc, fe, fw, fn, fs,
     io, go, gp, mx, ps, pr, hs, bsr, bmean, force, obs_in, msg, got,
-    c_a, c_u, c_v, s_obs1, r_obs1, s_obs2, r_obs2, s_v, r_v, s_h0, r_h0, s_h1, r_h1, s_pair, r_pair,
+    c_small, c_a, c_u, c_v, s_obs1, r_obs1, s_obs2, r_obs2, s_v, r_v, s_h0, r_h0, s_h1, r_h1, s_pair, r_pair,
     s_part, r_part, s_bs, r_bs, s_mean, r_mean,
 ):
     T, R, C, L, _ = a_ref.shape
@@ -125,6 +126,15 @@
         load_a(t).start()
 
     load_u.start()
+    small = [
+        pltpu.make_async_copy(src, dst, c_small.at[i])
+        for i, (src, dst) in enumerate((
+            (raw_values, values_ref), (raw_column, column_ref), (raw_count, count_ref),
+            (raw_inv, inv_ref), (raw_band, band_ref), (raw_flux, flux_ref),
+        ))
+    ]
+    for load in small:
+        load.start()
 
     barrier = pltpu.get_barrier_semaphore()
     for d in range(1, lat_n):
@@ -152,6 +162,9 @@
             for c in range(C):
                 a_ref[t, r, c] = staged[tile(r, c), :]
         halo_send(a_ref, halo0, s_h0, r_h0, t)
+
+    for load in small:
+        load.wait()
 
     slot = lax.broadcasted_iota(jnp.int32, (cap, cap), 0)
     across = lax.broadcasted_iota(jnp.int32, (cap, cap), 1)
@@ -326,11 +339,11 @@
             for c in range(C):
                 finished[tile(r, c), :] = acc[c]
 
-    stages = (stage_a, stage_b, stage_c, stage_d)
-
-    @pl.loop(0, T + len(stages) - 1)
+    stages = ((stage_d, 7), (stage_c, 5), (stage_b, 2), (stage_a, 0))
+
+    @pl.loop(0, T + 7)
     def _(s):
-        for lag, run in enumerate(stages):
+        for run, lag in stages:
             @pl.when(jnp.logical_and(s >= lag, s < T + lag))
             def _():
                 run(s - lag)
@@ -376,7 +389,9 @@
     f32 = jnp.float32
     vm = lambda *shape: pltpu.VMEM(shape, f32)
     dma = lambda *shape: pltpu.SemaphoreType.DMA(shape)
+    operands = (conv_band, mass_flux, diff_inverse, obs_values, obs_column)
     scratch = [
+        *[pltpu.VMEM(x.shape, x.dtype) for x in operands], pltpu.SMEM(obs_count.shape, obs_count.dtype),
         vm(T, L * K, LANES), vm(L * K, LANES), vm(L * K, LANES),
         vm(T, R, C, L, LANES), vm(R, C, L, LANES), vm(R, C, L, LANES),
         vm(R, size, L, LANES), vm(lat_n, cap, depth), vm(K, LANES),
@@ -386,22 +401,22 @@
         vm(R, C, 2 * L, LANES), vm(T, K, LANES), vm(T, K // 2, LANES), vm(T, K // 2, LANES),
         vm(chips - 1, T, K // 2, LANES), vm(T, K, LANES),
         vm(K, L, LANES), vm(width, depth), vm(lev_n, 2 * L, width), vm(lev_n, 2 * L, width),
-        dma(T), pltpu.SemaphoreType.DMA, pltpu.SemaphoreType.DMA,
+        dma(6), dma(T), pltpu.SemaphoreType.DMA, pltpu.SemaphoreType.DMA,
         dma(lat_n - 1), dma(lat_n - 1), dma(lev_n - 1), dma(lev_n - 1),
         pltpu.SemaphoreType.DMA, pltpu.SemaphoreType.DMA,
         dma(2, T), dma(2, T), dma(2, T), dma(2, T), dma(T), dma(T), dma(T), dma(T),
         dma(chips - 1, T), dma(chips - 1, T), dma(T), dma(T),
     ]
     vmem = pl.BlockSpec(memory_space=pltpu.VMEM)
-    hbm = pl.BlockSpec(memory_space=pl.ANY)
+    hbm = pl.BlockSpec(memory_space=pltpu.HBM)
     out = pl.pallas_call(
         functools.partial(kernel, lev_n, lat_n),
         out_shape=jax.ShapeDtypeStruct((T, L * K, LANES), f32),
-        in_specs=[hbm] * 3 + [vmem] * 5 + [pl.BlockSpec(memory_space=pltpu.SMEM)],
-        out_specs=pl.BlockSpec(memory_space=pltpu.VMEM),
+        in_specs=[hbm] * 9,
+        out_specs=vmem,
         scratch_shapes=scratch,
         compiler_params=pltpu.CompilerParams(
-            collective_id=0, has_side_effects=True, vmem_limit_bytes=44 * 1024 * 1024
+            collective_id=0, has_side_effects=True, vmem_limit_bytes=63 * 1024 * 1024
         ),
     )(a, u, v, conv_band, mass_flux, diff_inverse, obs_values, obs_column, obs_count)
     return out.reshape(T, L, C, R, LANES).transpose(0, 1, 3, 2, 4).reshape(T, L, R, lon)

time: 57.6 us -> 47.2 us (0.82)
  local copies, waits for them, and re-layouts: 9.4 us -> 3.16 us
  Pallas kernels: 47.5 us -> 43.7 us
    unnamed x19 -> x1, local copies, waits for them, and re-layouts: 9.4 us -> 3.16 us
    pallas_call x1, Pallas kernels: 47.5 us -> 43.7 us  [body(): pl.pallas_call(functools.partial(kernel, lev_n, lat_n), out_shape=jax.Sha...]
where the time goes in v3:
time: 47.2 us; the launch traced here: 46.8 us
  Pallas kernels  43.7 us (93%)
  local copies, waits for them, and re-layouts  3.16 us (7%)
    pallas_call x1, Pallas kernels, body(): pl.pallas_call(functools.partial(kernel, lev_n, lat_n), out_shape=jax.Sha...  43.7 us
    unnamed x1, local copies, waits for them, and re-layouts  3.16 us

profile of v3, /device:TPU:0, one launch (start us, length us, event | category | flops | bytes accessed | tf_op | source)
XLA Modules:
  0.0 46.8 jit_solution(3091182082153829269)
XLA Ops:
  0.0 43.7 %shard_map.91 = f32[8,512,128]{2,1,0:T(8,128)} custom-call(f32[8,512,128]{2,1,0:T(8,128)} %bitcast.21, f32[512,128]{1,0:T(8,128)} %bitcast.22, f32[512,128]{1,0:T(8,128)} %bitcast.23, s32[2,4,2048]{2,1,0:T(4,128)} %raw_band.1, f32[4,2048]{1,0:T(4,128)} %raw_flux.1, f32[4,4,16,16]{3,2,1,0:T(8,128)} %raw_inv.1, f32[1,1,4,16,64]{4,3,2,1,0:T(8,128)} %raw_values.1, ...), custom_call_target="tpu_custom_call" | custom-call | tf_op jit(solution)/shard_map/pallas_call | solution.py:412
  43.7 3.2 %copy.15 = f32[8,8,4,2048]{3,2,1,0:T(4,128)} copy(f32[8,8,4,2048]{3,2,1,0:T(4,128)} %bitcast.20) | data formatting | bytes 4194304
